TPU v7x, 128 devices: a whole 4x4x4 slice. The times are simulated.
128 devices in a mesh: row: 16 (over y_hi, x, core), col: 8 (over y_lo, z).
Axes of the slice: x: 4, y: 4 (y_hi: 2, y_lo: 2; y = y_hi * 2 + y_lo), z: 4, core: 2. Of those that a mesh axis runs over, the one named last changes fastest.
Arguments:
- genotypes: int32 [32768, 512], P(('row', 'col')), may hold values from 0 to 2, as said below
- pairs: int32 [128, 2, 2], replicated, may hold values from -1 to 15, as said below
Outputs:
- relation: bfloat16 [128, 2, 2048, 2048], P(('row', 'col'))
Inputs may be any that keep to these rules, and one draw needn't show every extreme that they name: `genotypes`: allele counts of one individual at one variant. `pairs`: each pair (r, j) of blocks with 0 <= j <= r < 16 stands in exactly one slot, as (r, j); every other slot holds (-1, -1).
All inputs are finite; a program needn't handle non-finite values.
Results may differ from a plain program's by a relative error of at most 0.0051.
Values may be sent and summed in bfloat16 or wider, within the bound.
A program may use at most 192 MiB of HBM per device.

v0:
```python
import jax
import jax.numpy as jnp
from jax import lax
from jax.sharding import PartitionSpec as P

SNPS = 512


def tile_block(left_panel, right_panel, is_live):
    product = lax.dot_general(
        left_panel, right_panel, (((1,), (1,)), ((), ())), preferred_element_type=jnp.float32
    )
    return jnp.where(is_live, product / SNPS, 0.0).astype(jnp.bfloat16)


def on_device(genotypes, pairs):
    counts = genotypes.astype(jnp.float32)
    row_count = lax.axis_size("row")
    col_count = lax.axis_size("col")
    shard_rows = counts.shape[0]
    sample_total = shard_rows * row_count * col_count
    mean_value = lax.psum(jnp.sum(counts, axis=0), ("row", "col")) / sample_total
    centered = counts - mean_value
    variance = lax.psum(jnp.sum(centered * centered, axis=0), ("row", "col")) / sample_total + 1e-05
    standard = (centered * lax.rsqrt(variance)).astype(jnp.bfloat16)
    variants = standard.shape[1]
    row_index = lax.axis_index("row")
    col_index = lax.axis_index("col")
    device = row_index * col_count + col_index
    own_pairs = lax.dynamic_index_in_dim(pairs, device, 0, keepdims=False)
    wanted_blocks = jnp.maximum(own_pairs.reshape(4), 0)
    everything = lax.all_gather(standard, ("row", "col"), axis=0, tiled=True)
    all_blocks = everything.reshape(row_count, shard_rows * col_count, variants)
    panels = jnp.take(all_blocks, wanted_blocks, axis=0)
    is_live = own_pairs[:, 0] >= 0
    first_tile = tile_block(panels[0], panels[1], is_live[0])
    second_tile = tile_block(panels[2], panels[3], is_live[1])
    return jnp.stack([first_tile, second_tile])[None]


def solution(mesh):
    in_specs = (P(("row", "col"), None), P())
    out_specs = P(("row", "col"), None, None, None)
    return jax.shard_map(
        on_device, mesh=mesh, in_specs=in_specs, out_specs=out_specs, check_vma=False
    )
```

profile of v0, /device:TPU:1, one launch (start us, length us, event | category | flops | bytes accessed | tf_op | source)
XLA Modules:
  0.0 563.1 jit_solution(16995358874965553574)
XLA Ops:
  6.5 0.0 all-gather.2.cloned.1.call-start
  6.5 1.1 convert_reduce_fusion
  7.6 68.7 %psum.14 = f32[512]{0:T(512)S(1)} all-reduce(f32[512]{0:T(512)S(1)} %convert_reduce_fusion), channel_id=1, replica_groups=mesh['row'=16,'col'=8] {'row','col'}, use_global_device_ids=true, to_apply=%region_1.0 | all-reduce | flops 512 | bytes 4096 | tf_op jit(solution)/shard_map/psum | solution.py:22
  76.3 1.1 multiply_reduce_fusion
  77.5 62.6 %psum.15 = f32[512]{0:T(512)S(1)} all-reduce(f32[512]{0:T(512)S(1)} %multiply_reduce_fusion), channel_id=1, replica_groups=mesh['row'=16,'col'=8] {'row','col'}, use_global_device_ids=true, to_apply=%region_3.0 | all-reduce | flops 512 | bytes 4096 | tf_op jit(solution)/shard_map/psum | solution.py:24
  140.1 1.8 multiply_convert_fusion
  141.9 0.0 all-gather.2.cloned.1.call-update
  141.9 0.9 maximum_reduce_fusion
  142.8 0.1 reshape.38
  142.9 0.9 compare_reduce_fusion
  143.8 0.1 le.11
  143.9 0.6 fusion.3
  144.5 343.5 %all-gather.2.cloned.1.call-done = bf16[32768,512]{1,0:T(8,128)(2,1)} async-done(((bf16[256,512]{1,0:T(8,128)(2,1)}), bf16[32768,512]{1,0:T(8,128)(2,1)}) %all-gather.2.cloned.1.call-update) | async-done | bytes 33554448 | tf_op jit(solution)/shard_map/all_gather | solution.py:32
  488.0 22.6 %fusion.2 = (bf16[16,1024,512]{2,1,0:T(8,128)(2,1)}, bf16[16,1024,512]{2,1,0:T(8,128)(2,1)}) fusion(bf16[16,2048,512]{2,1,0:T(8,128)(2,1)} %bitcast.21), kind=kLoop, calls=%fused_computation.23 | loop fusion | bytes 67108864 | tf_op jit(solution)/shard_map/jit(_take)/gather | solution.py:34
  510.7 8.5 %gather_fusion.1 = bf16[4,1024,512]{2,1,0:T(8,128)(2,1)} fusion(bf16[16,1024,512]{2,1,0:T(8,128)(2,1)} %get-tuple-element.8, s32[1024]{0:T(1024)S(1)} %pad_clamp_fusion), kind=kCustom, calls=%fused_computation.1 | custom fusion | bytes 8388624 | tf_op jit(solution)/shard_map/jit(_take)/gather | solution.py:34
  519.2 8.6 %gather_fusion = bf16[4,1024,512]{2,1,0:T(8,128)(2,1)} fusion(bf16[16,1024,512]{2,1,0:T(8,128)(2,1)} %get-tuple-element.7, s32[1024]{0:T(1024)S(1)} %pad_clamp_fusion), kind=kCustom, calls=%fused_computation | custom fusion | bytes 8388624 | tf_op jit(solution)/shard_map/jit(_take)/gather | solution.py:34
  527.7 5.1 maximum_select_fusion
  532.9 5.5 fusion.1
  538.3 7.5 %fusion = bf16[1,2048,2048]{2,1,0:T(8,128)(2,1)} fusion(pred[]{:T(512)} %bitcast, bf16[4,2048,512]{2,1,0:T(8,128)(2,1)S(1)} %maximum_select_fusion), kind=kOutput, calls=%fused_computation.6 | convolution fusion | flops 4307550208 | bytes 12582913 | tf_op jit(solution)/shard_map/dot_general | solution.py:10
  545.8 10.5 %maximum_bitcast_fusion = bf16[1,2,2048,2048]{3,2,1,0:T(8,128)(2,1)} fusion(bf16[1,2048,2048]{2,1,0:T(8,128)(2,1)S(1)} %fusion.1, bf16[1,2048,2048]{2,1,0:T(8,128)(2,1)} %fusion), kind=kLoop, calls=%fused_computation.2 | loop fusion | flops 8388608 | bytes 33554432 | tf_op jit(solution)/shard_map/broadcast_in_dim | solution.py:38
  (4 shorter events, 0.0 us)
Async XLA Ops:
  6.5 481.5 %all-gather.2.cloned.1.call-start = ((), (), s32[]{:S(2)}) async-start(), calls=%async_computation | async-start | bytes 33816576 | tf_op jit(solution)/shard_map/all_gather | solution.py:32
Sparse Core Ops, SparseCore 0:
  142.1 345.9 all-gather.1
where the time goes:
time: 564 us; the launch traced here: 563 us
  waiting for transfers between devices  344 us (61%)
  blocking collectives  131 us (23%)
  local copies, waits for them, and re-layouts  40.4 us (7%)
  other arithmetic  21.5 us (4%)
  between operations  13.4 us (2%)
  matrix products  12.9 us (2%)
    all_gather x1, waiting for transfers between devices, on_device(): everything = lax.all_gather(standard, ('row', 'col'), axis=0, tiled=True)  344 us
    psum x1, blocking collectives, on_device(): lax.psum(jnp.sum(counts, axis=0), ('row', 'col')) / sample_total  68.7 us
    psum x1, blocking collectives, on_device(): lax.psum(jnp.sum(centered * centered, axis=0), ('row', 'col'))  62.6 us
    gather x3, local copies, waits for them, and re-layouts, on_device(): panels = jnp.take(all_blocks, wanted_blocks, axis=0)  39.7 us
    dot_general x2, matrix products, tile_block(): lax.dot_general(left_panel, right_panel, (((1,), (1,)), ((), ())), prefer...  12.9 us
  transfers between devices with their start and end apart: 1, of which 1 were waited for; matrix products, arithmetic and copies ran while one was open for 0% of the time, Pallas kernels for 0%

commit v1 on v0

v1 whole, which is shorter than its diff:
```python
import functools
import itertools
import random

import jax
import jax.numpy as jnp
from jax import lax
from jax.experimental import pallas as pl
from jax.experimental.pallas import tpu as pltpu
from jax.sharding import PartitionSpec as P

MESH = pl.DeviceIdType.MESH
SNPS = 512
RING = 4
ROW_COUNT = 16
COL_COUNT = 8
SHARD = 256
SAMPLES = SHARD * ROW_COUNT * COL_COUNT
BLOCK = SHARD * COL_COUNT
PARTS = 2
PIECE = SHARD // PARTS
LINKS = ((1, 0, 0), (3, 0, 0), (0, 1, 0), (0, 3, 0), (0, 0, 1), (0, 0, 3))
OFFSETS = tuple(itertools.product(range(RING), repeat=3))
STAT_HOPS = {0: ("core",), 1: (1, 0, 0), 2: (0, 1, 0), 3: (0, 0, 1)}
CHUNK = 256


def plus(a, b):
    return tuple((i + j) % RING for i, j in zip(a, b))


def minus(a, b):
    return tuple((i - j) % RING for i, j in zip(a, b))


def number(offset):
    return (offset[0] * RING + offset[1]) * RING + offset[2]


def hops(offset):
    return sum(min(i, RING - i) for i in offset)


def attempt(seed, lag):
    rnd = random.Random(seed)
    have = {(p, (0, 0, 0)): -lag for p in range(PARTS)}
    steps = []
    for t in range((len(OFFSETS) - 1) * PARTS // len(LINKS)):
        choices = []
        for link in LINKS:
            ready = [
                (p, d)
                for p in range(PARTS)
                for d in OFFSETS
                if (p, d) not in have and have.get((p, minus(d, link)), t) <= t - lag
            ]
            rnd.shuffle(ready)
            ready.sort(key=lambda job: hops(job[1]))
            choices.append(ready)
        taken = {}

        def place(link, seen):
            for job in choices[link]:
                if job not in seen:
                    seen.add(job)
                    if job not in taken or place(taken[job], seen):
                        taken[job] = link
                        return True
            return False

        for link in range(len(LINKS)):
            if not place(link, set()):
                return None
        steps.append(sorted((link, p, d) for (p, d), link in taken.items()))
        have.update({job: t for job in taken})
    return steps


@functools.cache
def schedule():
    return next(s for s in (attempt(seed, 2) for seed in range(1000)) if s is not None)


def place_of_self():
    row, col = lax.axis_index("row"), lax.axis_index("col")
    return (row // 2) % RING, (row // 8) * 2 + col // RING, col % RING, row % 2


def gather_kernel(
    counts_ref, all_ref, stat_ref, own, sums, own_sem, send_sem, recv_sem, twin_send, twin_recv, stat_send, stat_recv
):
    x, y, z, core = place_of_self()

    def device_at(offset, same_core=True):
        px, py, pz = ((me + step) % RING for me, step in zip((x, y, z), offset))
        return ((py // 2) * RING + px) * 2 + (core if same_core else 1 - core), (py % 2) * RING + pz

    twin = device_at((0, 0, 0), False)
    neighbours = [device_at(link) for link in LINKS]
    across = {axis: device_at(tuple(2 * (a == axis) for a in range(3))) for axis in range(3)}

    barrier = pltpu.get_barrier_semaphore()
    peers = [twin, *neighbours, *across.values()]
    for peer in peers:
        pl.semaphore_signal(barrier, inc=1, device_id=peer, device_id_type=MESH)
    counts = counts_ref[...]
    own[...] = counts.astype(jnp.float32).astype(jnp.bfloat16)
    pl.semaphore_wait(barrier, len(peers))

    zero = (0, 0, 0)

    def piece(p, offset):
        if offset == zero:
            return own.at[pl.ds(p * PIECE, PIECE)]
        return all_ref.at[p, number(offset), 0]

    def over_link(link, p, offset):
        n = number(offset)
        return pltpu.make_async_remote_copy(
            src_ref=piece(p, minus(offset, LINKS[link])),
            dst_ref=all_ref.at[p, n, 0],
            send_sem=send_sem.at[p, n],
            recv_sem=recv_sem.at[p, n],
            device_id=neighbours[link],
            device_id_type=MESH,
        )

    def to_twin(p, offset):
        n = number(offset)
        return pltpu.make_async_remote_copy(
            src_ref=piece(p, offset),
            dst_ref=all_ref.at[p, n, 1],
            send_sem=twin_send.at[p, n],
            recv_sem=twin_recv.at[p, n],
            device_id=twin,
            device_id_type=MESH,
        )

    def sum_to(slot, source, target):
        return pltpu.make_async_remote_copy(
            src_ref=sums.at[source],
            dst_ref=sums.at[slot],
            send_sem=stat_send.at[slot],
            recv_sem=stat_recv.at[slot],
            device_id=target,
            device_id_type=MESH,
        )

    def stat_copies(phase):
        if phase == 0:
            return [sum_to(1, 0, twin)]
        axis, base = phase - 1, 4 * phase - 2
        targets = [neighbours[2 * axis], neighbours[2 * axis + 1], across[axis]]
        return [sum_to(base + 1 + i, base, target) for i, target in enumerate(targets)]

    def stat_finish(phase):
        for copy in stat_copies(phase):
            copy.wait()
        if phase == 0:
            sums[2] = sums[0] + sums[1]
        else:
            base = 4 * phase - 2
            sums[base + 4] = (sums[base] + sums[base + 1]) + (sums[base + 2] + sums[base + 3])

    steps = schedule()
    arrived = {(p, zero) for p in range(PARTS)}

    def arrive(link, p, offset):
        if (p, offset) not in arrived:
            arrived.add((p, offset))
            over_link(link, p, offset).wait_recv()
            to_twin(p, offset).start()

    came_by = {(p, offset): link for step in steps for link, p, offset in step}
    for t, step in enumerate(steps):
        for link, p, offset in step:
            source = minus(offset, LINKS[link])
            arrive(came_by.get((p, source)), p, source)
            over_link(link, p, offset).start()
        if t == 1:
            for p in range(PARTS):
                to_twin(p, zero).start()
                pltpu.make_async_copy(piece(p, zero), all_ref.at[p, 0, 0], own_sem.at[p]).start()
            total = jnp.sum(counts, axis=0, keepdims=True)
            square = jnp.sum(counts * counts, axis=0, keepdims=True)
            which = lax.broadcasted_iota(jnp.int32, (8, SNPS), 0)
            sums[0] = jnp.where(which == 0, total, jnp.where(which == 1, square, 0))
            for copy in stat_copies(0):
                copy.start()
        if t in (4, 6, 8, 10):
            phase = (t - 4) // 2
            stat_finish(phase)
            if phase < 3:
                for copy in stat_copies(phase + 1):
                    copy.start()

    total, square = sums[14, 0:1], sums[14, 1:2]
    shifted = total - SAMPLES
    spread = SAMPLES * (square - 2 * total + SAMPLES) - shifted * shifted
    variance = spread.astype(jnp.float32) * (1.0 / (float(SAMPLES) * SAMPLES)) + 1e-05
    mean = total.astype(jnp.float32) * (1.0 / SAMPLES)
    which = lax.broadcasted_iota(jnp.int32, (8, SNPS), 0)
    stat_ref[...] = jnp.where(which == 0, mean, lax.rsqrt(variance))

    for step in steps:
        for link, p, offset in step:
            arrive(link, p, offset)
    for p in range(PARTS):
        pltpu.make_async_copy(piece(p, zero), all_ref.at[p, 0, 0], own_sem.at[p]).wait()
        to_twin(p, zero).wait()
    for step in steps:
        for link, p, offset in step:
            over_link(link, p, offset).wait_send()
            to_twin(p, offset).wait()


def gather(counts):
    slots = (PARTS, len(OFFSETS))
    dma = pltpu.SemaphoreType.DMA
    return pl.pallas_call(
        gather_kernel,
        out_shape=(
            jax.ShapeDtypeStruct((*slots, 2, PIECE, SNPS), jnp.bfloat16),
            jax.ShapeDtypeStruct((8, SNPS), jnp.float32),
        ),
        in_specs=[pl.BlockSpec(memory_space=pltpu.VMEM)],
        out_specs=(pl.BlockSpec(memory_space=pl.ANY), pl.BlockSpec(memory_space=pltpu.VMEM)),
        scratch_shapes=[
            pltpu.VMEM((SHARD, SNPS), jnp.bfloat16),
            pltpu.VMEM((15, 8, SNPS), jnp.int32),
            dma((PARTS,)),
            dma(slots),
            dma(slots),
            dma(slots),
            dma(slots),
            dma((15,)),
            dma((15,)),
        ],
        name="gather_counts",
        compiler_params=pltpu.CompilerParams(
            collective_id=0, has_side_effects=True, vmem_limit_bytes=56 * 2**20
        ),
    )(counts)


def tile_kernel(want_ref, stat_ref, all_ref, out_ref, panels, sem):
    slot, chunk = pl.program_id(0), pl.program_id(1)
    x, y, z, core = place_of_self()
    mean, scale = stat_ref[0:1], stat_ref[1:2]

    def copies(panel, col):
        block = jnp.maximum(want_ref[panel], 0)
        behind = (
            ((x - (block // 2) % RING) % RING) * RING + (y - (block // 8) * 2 - col // RING) % RING
        ) * RING + (z - col % RING) % RING
        other = jnp.where(block % 2 == core, 0, 1)
        return [
            pltpu.make_async_copy(
                all_ref.at[p, behind, other],
                panels.at[panel, pl.ds(col * SHARD + p * PIECE, PIECE)],
                sem.at[panel, col, p],
            )
            for p in range(PARTS)
        ]

    def fetch(panel):
        def one(col, carry):
            for copy in copies(panel, col):
                copy.start()
            return carry

        lax.fori_loop(0, COL_COUNT, one, 0)

    def standardize(panel, col):
        for copy in copies(panel, col):
            copy.wait()
        rows = pl.ds(col * SHARD, SHARD)
        counts = panels[panel, rows].astype(jnp.float32)
        panels[panel, rows] = ((counts - mean) * scale).astype(jnp.bfloat16)

    def live(which):
        return want_ref[2 * which] >= 0

    @pl.when((slot == 0) & (chunk == 0))
    def _():
        for which in range(2):

            @pl.when(live(which))
            def _():
                fetch(2 * which + 1)
                fetch(2 * which)

    @pl.when((slot == 0) & (chunk == 0) & live(0))
    def _():
        lax.fori_loop(0, COL_COUNT, lambda col, c: (standardize(1, col), c)[1], 0)

    @pl.when((slot == 0) & live(1))
    def _():
        standardize(3, chunk)

    @pl.when(live(slot))
    def _():
        standardize(2 * slot, chunk)
        left = panels[2 * slot, pl.ds(chunk * CHUNK, CHUNK)]
        product = lax.dot_general(
            left, panels[2 * slot + 1], (((1,), (1,)), ((), ())), preferred_element_type=jnp.float32
        )
        out_ref[0, 0] = (product * (1.0 / SNPS)).astype(jnp.bfloat16)

    @pl.when(jnp.logical_not(live(slot)))
    def _():
        out_ref[0, 0] = jnp.zeros((CHUNK, BLOCK), jnp.bfloat16)


def tiles(want, stats, everything):
    return pl.pallas_call(
        tile_kernel,
        out_shape=jax.ShapeDtypeStruct((1, 2, BLOCK, BLOCK), jnp.bfloat16),
        grid_spec=pltpu.PrefetchScalarGridSpec(
            num_scalar_prefetch=1,
            grid=(2, BLOCK // CHUNK),
            in_specs=[
                pl.BlockSpec((8, SNPS), lambda s, i, w: (0, 0)),
                pl.BlockSpec(memory_space=pl.ANY),
            ],
            out_specs=pl.BlockSpec((1, 1, CHUNK, BLOCK), lambda s, i, w: (0, s, i, 0)),
            scratch_shapes=[
                pltpu.VMEM((4, BLOCK, SNPS), jnp.bfloat16),
                pltpu.SemaphoreType.DMA((4, COL_COUNT, PARTS)),
            ],
        ),
        name="tile_products",
        compiler_params=pltpu.CompilerParams(vmem_limit_bytes=48 * 2**20),
    )(want, stats, everything)


def on_device(genotypes, pairs):
    everything, stats = gather(genotypes)
    device = lax.axis_index("row") * COL_COUNT + lax.axis_index("col")
    want = lax.dynamic_index_in_dim(pairs, device, 0, keepdims=False).reshape(4)
    return tiles(want, stats, everything)


def solution(mesh):
    return jax.shard_map(
        on_device,
        mesh=mesh,
        in_specs=(P(("row", "col"), None), P()),
        out_specs=P(("row", "col"), None, None, None),
        check_vma=False,
    )
```

time: 564 us -> 107 us (0.19)
  the two profiles are of different devices: /device:TPU:1 before, /device:TPU:3 now
where the time goes in v1:
time: 107 us
  Pallas kernels  105 us (98%)
  local copies, waits for them, and re-layouts  1.69 us (2%)
    pallas_call x1, Pallas kernels, gather(): pl.pallas_call(gather_kernel, out_shape=(jax.ShapeDtypeStruct((*slots, 2,...  84.7 us
    pallas_call x1, Pallas kernels, tiles(): pl.pallas_call(tile_kernel, out_shape=jax.ShapeDtypeStruct((1, 2, BLOCK,...  20.5 us

profile of v1, /device:TPU:3, one launch (start us, length us, event | category | flops | bytes accessed | tf_op | source)
XLA Modules:
  0.0 106.8 jit_solution(8907054798482637126)
XLA Ops:
  0.0 0.0 copy-start
  0.0 0.7 copy-done
  0.7 0.2 dynamic-slice_reduce_fusion
  0.9 0.1 reshape.4.want_ref
  1.0 84.7 %gather_counts.1 = (bf16[2,64,2,128,512]{4,3,2,1,0:T(8,128)(2,1)}, f32[8,512]{1,0:T(8,128)}) custom-call(s32[256,512]{1,0:T(8,128)} %counts_ref.1), custom_call_target="tpu_custom_call" | custom-call | tf_op jit(solution)/shard_map/gather_counts/pallas_call | solution.py:220
  85.6 0.0 copy-start.1
  85.7 0.7 copy-done.1
  86.4 20.5 %tile_products.1 = bf16[1,2,2048,2048]{3,2,1,0:T(8,128)(2,1)} custom-call(s32[4]{0:T(128)S(1)} %reshape.4.want_ref, f32[8,512]{1,0:T(8,128)S(1)} %copy-done.1, bf16[2,64,2,128,512]{4,3,2,1,0:T(8,128)(2,1)} %get-tuple-element.8.all_ref), custom_call_target="tpu_custom_call" | custom-call | tf_op jit(solution)/shard_map/tile_products/pallas_call | solution.py:316
Async XLA Ops:
  0.0 0.7 copy-start
  85.6 0.7 copy-start.1

commit v2 on v0

v2 whole, which is shorter than its diff:
```python
import jax
import jax.numpy as jnp
import numpy as np
from jax import lax
from jax.experimental import pallas as pl
from jax.experimental.pallas import tpu as pltpu
from jax.sharding import PartitionSpec as P

MESH = pl.DeviceIdType.MESH
SNPS = 512
RING = 4
ROW_COUNT = 16
COL_COUNT = 8
SHARD = 256
SAMPLES = SHARD * ROW_COUNT * COL_COUNT
BLOCK = SHARD * COL_COUNT
STREAMS = 2
PARTS = 2
PIECE = SHARD // (STREAMS * PARTS)
PANELS = 4
LINKS = ((1, 0, 0), (3, 0, 0), (0, 1, 0), (0, 3, 0), (0, 0, 1), (0, 0, 3))
PER_LINK = 2
CHUNK = 512

RELAYS = (
    ((1, 16), (0, 48), (0, 4), (1, 12), (0, 1), (0, 3)),
    ((0, 20), (0, 32), (0, 8), (0, 15), (1, 13), (1, 3)),
    ((0, 24), (0, 56), (1, 7), (0, 44), (0, 21), (0, 14)),
    ((0, 30), (1, 61), (1, 20), (0, 10), (0, 22), (0, 47)),
    ((0, 38), (1, 45), (0, 18), (1, 57), (0, 57), (1, 6)),
    ((1, 19), (1, 51), (1, 10), (1, 41), (0, 39), (0, 46)),
    ((1, 35), (0, 49), (1, 55), (1, 31), (1, 42), (0, 29)),
)
DIRECT = (
    ((0, 9), (0, 19), (0, 34), (0, 40), (0, 45), (0, 54), (0, 55), (0, 62), (0, 63), (1, 9), (1, 22), (1, 26), (1, 29), (1, 36)),
    ((0, 6), (0, 16), (0, 23), (0, 28), (0, 33), (0, 41), (1, 4), (1, 15), (1, 25), (1, 39), (1, 48), (1, 54), (1, 58), (1, 60)),
    ((0, 7), (0, 26), (0, 35), (0, 42), (0, 43), (0, 53), (0, 61), (1, 1), (1, 24), (1, 33), (1, 49), (1, 59)),
    ((0, 12), (0, 17), (0, 52), (0, 60), (1, 2), (1, 8), (1, 27), (1, 28), (1, 37), (1, 38), (1, 47), (1, 53), (1, 63)),
    ((0, 5), (0, 25), (0, 31), (0, 36), (0, 50), (0, 58), (1, 11), (1, 14), (1, 17), (1, 21), (1, 32), (1, 43), (1, 46), (1, 52), (1, 62)),
    ((0, 2), (0, 11), (0, 13), (0, 27), (0, 37), (0, 51), (0, 59), (1, 5), (1, 18), (1, 23), (1, 30), (1, 34), (1, 40), (1, 44), (1, 50), (1, 56)),
)

def offset_of(n):
    return n // (RING * RING), n // RING % RING, n % RING


def number(offset):
    return (offset[0] * RING + offset[1]) * RING + offset[2]


def before(n, link):
    return number(tuple((i - j) % RING for i, j in zip(offset_of(n), LINKS[link])))


HELD = tuple((p, 0) for p in range(PARTS)) + tuple(item for step in RELAYS for item in step)
SLOT_OF = {item: i for i, item in enumerate(HELD)}
CAME_BY = {item: link for step in RELAYS for link, item in enumerate(step)}


def class_of(n, y_lo):
    dx, dy, _ = offset_of(n)
    return (dx * 2 + y_lo) * 2 + ((dy + 1 - y_lo) // 2) % 2


def tables():
    lists = {}
    for y_lo in range(2):
        for c in range(RING):
            for half in range(2):
                kind = (c * 2 + y_lo) * 2 + half
                links = [
                    [(SLOT_OF[p, before(n, e)], p, n) for p, n in DIRECT[e] if class_of(n, y_lo) == kind]
                    for e in range(len(LINKS))
                ]
                own = [(i, p, n) for i, (p, n) in enumerate(HELD) if class_of(n, y_lo) == kind]
                lists[kind] = (links, own)
    assert all(len(part) <= PER_LINK for links, _ in lists.values() for part in links)
    own_most = max(len(own) for _, own in lists.values())
    pieces = len(LINKS) * PER_LINK + own_most
    slots = np.zeros((len(lists), pieces), np.int32)
    items = np.full((len(lists), pieces), -1, np.int32)
    for kind, (links, own) in lists.items():
        for base, part in [(e * PER_LINK, part) for e, part in enumerate(links)] + [(len(links) * PER_LINK, own)]:
            for i, (slot, p, n) in enumerate(part):
                slots[kind, base + i] = slot
                items[kind, base + i] = p * RING**3 + n
    return slots, items, own_most


SLOTS, ITEMS, OWN = tables()
FROM_LINKS = len(LINKS) * PER_LINK
PIECES = FROM_LINKS + OWN


def place_of_self():
    row, col = lax.axis_index("row"), lax.axis_index("col")
    return (row // 2) % RING, (row // 8) * 2 + col // RING, col % RING, row % 2


def kind_of(block, x, y):
    behind = (x - lax.shift_right_logical(block, 1)) & (RING - 1)
    half = ((y // 2) - lax.shift_right_logical(block, 3)) & 1
    return (behind * 2 + y % 2) * 2 + half


def gather_kernel(
    counts_ref, pairs_ref, slots_ref, out_ref,
    held, sums, away, near,
    twin_send, twin_recv, relay_send, relay_recv, stat_send, stat_recv,
    link_send, link_recv, near_send, near_recv, own_sem,
):
    x, y, z, core = place_of_self()

    def place(offset):
        return tuple((me + step) % RING for me, step in zip((x, y, z), offset))

    def device_at(offset, on_core):
        px, py, pz = place(offset)
        return ((py // 2) * RING + px) * 2 + on_core, (py % 2) * RING + pz

    twin = device_at((0, 0, 0), 1 - core)
    neighbours = [device_at(link, core) for link in LINKS]
    across = [device_at(tuple(2 * (a == axis) for a in range(3)), core) for axis in range(3)]
    others = [device_at(link, 1 - core) for link in LINKS]

    barrier = pltpu.get_barrier_semaphore()
    peers = [twin, *neighbours, *others, *across]
    for peer in peers:
        pl.semaphore_signal(barrier, inc=1, device_id=peer, device_id_type=MESH)

    def as_bf16(first, rows):
        return counts_ref[pl.ds(first, rows)].astype(jnp.float32).astype(jnp.bfloat16)

    mine, theirs = core * (SHARD // 2), (1 - core) * (SHARD // 2)
    for p in range(PARTS):
        near[0, p] = as_bf16(pl.multiple_of(theirs + p * PIECE, PIECE), PIECE)
        held[p, core] = as_bf16(pl.multiple_of(mine + p * PIECE, PIECE), PIECE)
    pl.semaphore_wait(barrier, len(peers))

    def swap(p):
        return pltpu.make_async_remote_copy(
            src_ref=near.at[0, p],
            dst_ref=held.at[p, core],
            send_sem=twin_send.at[p],
            recv_sem=twin_recv.at[p],
            device_id=twin,
            device_id_type=MESH,
        )

    def swapped(p):
        return pltpu.make_async_remote_copy(
            src_ref=near.at[0, p],
            dst_ref=held.at[p, 1 - core],
            send_sem=twin_send.at[p],
            recv_sem=twin_recv.at[p],
            device_id=twin,
            device_id_type=MESH,
        )

    for p in range(PARTS):
        swap(p).start()

    def sum_to(slot, source, target):
        return pltpu.make_async_remote_copy(
            src_ref=sums.at[source],
            dst_ref=sums.at[slot],
            send_sem=stat_send.at[slot],
            recv_sem=stat_recv.at[slot],
            device_id=target,
            device_id_type=MESH,
        )

    def stat_copies(phase):
        if phase == 0:
            return [sum_to(1, 0, twin)]
        axis, base = phase - 1, 4 * phase - 2
        targets = [neighbours[2 * axis], neighbours[2 * axis + 1], across[axis]]
        return [sum_to(base + 1 + i, base, target) for i, target in enumerate(targets)]

    def stat_finish(phase):
        for copy in stat_copies(phase):
            copy.wait()
        if phase == 0:
            sums[2] = sums[0] + sums[1]
        else:
            base = 4 * phase - 2
            sums[base + 4] = (sums[base] + sums[base + 1]) + (sums[base + 2] + sums[base + 3])

    def stat_start():
        counts = counts_ref[...]
        total = jnp.sum(counts, axis=0, keepdims=True)
        square = jnp.sum(counts * counts, axis=0, keepdims=True)
        which = lax.broadcasted_iota(jnp.int32, (8, SNPS), 0)
        sums[0] = jnp.where(which == 0, total, jnp.where(which == 1, square, 0))
        for copy in stat_copies(0):
            copy.start()

    def relay(item, half):
        slot, link = SLOT_OF[item], CAME_BY[item]
        source = SLOT_OF[item[0], before(item[1], link)]
        return pltpu.make_async_remote_copy(
            src_ref=held.at[source, half],
            dst_ref=held.at[slot, half],
            send_sem=relay_send.at[slot, half],
            recv_sem=relay_recv.at[slot, half],
            device_id=neighbours[link],
            device_id_type=MESH,
        )

    arrived = set()

    def arrive(item, half):
        if (item, half) not in arrived:
            arrived.add((item, half))
            relay(item, half).wait_recv()

    for p in range(PARTS):
        swap(p).wait_send()
        swapped(p).wait_recv()
        arrived.update(((p, 0), half) for half in range(2))
    for t, step in enumerate(RELAYS):
        for half in range(2):
            for link, item in enumerate(step):
                arrive((item[0], before(item[1], link)), half)
                relay(item, half).start()
            if t == 0 and half == 0:
                stat_start()
        if 0 < t < 5:
            stat_finish(t - 1)
            if t < 4:
                for copy in stat_copies(t):
                    copy.start()
    for step in RELAYS:
        for half in range(2):
            for item in step:
                arrive(item, half)

    total, square = sums[14, 0:1], sums[14, 1:2]
    shifted = total - SAMPLES
    spread = SAMPLES * (square - 2 * total + SAMPLES) - shifted * shifted
    variance = spread.astype(jnp.float32) * (1.0 / (float(SAMPLES) * SAMPLES)) + 1e-05
    mean = total.astype(jnp.float32) * (1.0 / SAMPLES)
    scale = lax.rsqrt(variance)

    def standard(slot, half, factor):
        return ((held[slot, half].astype(jnp.float32) - mean) * (scale * factor)).astype(jnp.bfloat16)

    def wanted(device, panel):
        return jnp.maximum(pairs_ref[panel, device[0] * COL_COUNT + device[1]], 0)

    def to_link(link, to_core, panel):
        return pltpu.make_async_remote_copy(
            src_ref=away.at[link, to_core, panel],
            dst_ref=out_ref.at[panel, core, pl.ds(link * PER_LINK, PER_LINK)],
            send_sem=link_send.at[link, to_core, panel],
            recv_sem=link_recv.at[link, core, panel],
            device_id=device_at(LINKS[link], to_core),
            device_id_type=MESH,
        )

    def from_link(link, stream, panel):
        return pltpu.make_async_remote_copy(
            src_ref=away.at[link, 0, panel],
            dst_ref=out_ref.at[panel, stream, pl.ds(link * PER_LINK, PER_LINK)],
            send_sem=link_send.at[link, 0, panel],
            recv_sem=link_recv.at[link, stream, panel],
            device_id=neighbours[link],
            device_id_type=MESH,
        )

    def to_twin(panel, stream):
        return pltpu.make_async_remote_copy(
            src_ref=near.at[1 + panel, pl.ds(0, OWN)],
            dst_ref=out_ref.at[panel, stream, pl.ds(FROM_LINKS, OWN)],
            send_sem=near_send.at[panel],
            recv_sem=near_recv.at[panel],
            device_id=twin,
            device_id_type=MESH,
        )

    def to_self(panel):
        return pltpu.make_async_copy(
            near.at[1 + PANELS + panel, pl.ds(0, OWN)],
            out_ref.at[panel, core, pl.ds(FROM_LINKS, OWN)],
            own_sem.at[panel],
        )

    def send_panel(panel, carry):
        factor = jnp.where(panel % 2 == 0, 1.0 / SNPS, 1.0).astype(jnp.float32)
        for to_core in range(2):
            for link, step in enumerate(LINKS):
                block = wanted(device_at(step, to_core), panel)
                px, py, _ = place(step)
                kind = kind_of(block, px, py)
                for i in range(PER_LINK):
                    slot = slots_ref[kind, link * PER_LINK + i]
                    away[link, to_core, panel, i] = standard(slot, block & 1, factor)
                to_link(link, to_core, panel).start()
        for which, device in enumerate((twin, device_at((0, 0, 0), core))):
            block = wanted(device, panel)
            kind = kind_of(block, x, y)

            def one(i, c):
                slot = slots_ref[kind, FROM_LINKS + i]
                near[1 + which * PANELS + panel, i] = standard(slot, block & 1, factor)
                return c

            lax.fori_loop(0, OWN, one, 0)
            if which == 0:
                to_twin(panel, core).start()
            else:
                to_self(panel).start()
        return carry

    lax.fori_loop(0, PANELS, send_panel, 0)

    def finish_panel(panel, carry):
        for half in range(2):
            for link in range(len(LINKS)):
                to_link(link, half, panel).wait_send()
                from_link(link, half, panel).wait_recv()
        to_twin(panel, core).wait_send()
        to_twin(panel, 1 - core).wait_recv()
        to_self(panel).wait()
        return carry

    for step in RELAYS:
        for half in range(2):
            for item in step:
                relay(item, half).wait_send()
    lax.fori_loop(0, PANELS, finish_panel, 0)


def gather(counts, pairs):
    dma = pltpu.SemaphoreType.DMA
    return pl.pallas_call(
        gather_kernel,
        out_shape=jax.ShapeDtypeStruct((PANELS, STREAMS, PIECES, PIECE, SNPS), jnp.bfloat16),
        in_specs=[
            pl.BlockSpec(memory_space=pltpu.VMEM),
            pl.BlockSpec(memory_space=pltpu.SMEM),
            pl.BlockSpec(memory_space=pltpu.SMEM),
        ],
        out_specs=pl.BlockSpec(memory_space=pl.ANY),
        scratch_shapes=[
            pltpu.VMEM((len(HELD), 2, PIECE, SNPS), jnp.bfloat16),
            pltpu.VMEM((15, 8, SNPS), jnp.int32),
            pltpu.VMEM((len(LINKS), 2, PANELS, PER_LINK, PIECE, SNPS), jnp.bfloat16),
            pltpu.VMEM((1 + 2 * PANELS, max(OWN, PARTS), PIECE, SNPS), jnp.bfloat16),
            dma((PARTS,)),
            dma((PARTS,)),
            dma((len(HELD), 2)),
            dma((len(HELD), 2)),
            dma((15,)),
            dma((15,)),
            dma((len(LINKS), 2, PANELS)),
            dma((len(LINKS), 2, PANELS)),
            dma((PANELS,)),
            dma((PANELS,)),
            dma((PANELS,)),
        ],
        name="gather_panels",
        compiler_params=pltpu.CompilerParams(
            collective_id=0, has_side_effects=True, vmem_limit_bytes=56 * 2**20
        ),
    )(counts, pairs, jnp.asarray(SLOTS))


def tile_kernel(pairs_ref, items_ref, all_ref, out_ref, panels, sem):
    slot, chunk = pl.program_id(0), pl.program_id(1)
    x, y, z, core = place_of_self()
    device = lax.axis_index("row") * COL_COUNT + lax.axis_index("col")

    def fetch(panel):
        block = jnp.maximum(pairs_ref[panel, device], 0)
        kind = kind_of(block, x, y)

        def one(i, carry):
            item = items_ref[kind, i]

            @pl.when(item >= 0)
            def _():
                oy = (y - (item // RING)) & (RING - 1)
                oz = (z - item) & (RING - 1)
                first = ((oy & 1) * RING + oz) * SHARD + (item // RING**3) * PIECE
                for stream in range(STREAMS):
                    rows = pl.ds(pl.multiple_of(first + stream * (SHARD // 2), PIECE), PIECE)
                    pltpu.make_async_copy(all_ref.at[panel, stream, i], panels.at[panel, rows], sem.at[panel]).start()

            return carry

        lax.fori_loop(0, PIECES, one, 0)

    def arrive(panel):
        pltpu.make_async_copy(panels.at[panel], panels.at[panel], sem.at[panel]).wait()

    def live(which):
        return pairs_ref[2 * which, device] >= 0

    @pl.when((slot == 0) & (chunk == 0))
    def _():
        for which in range(2):

            @pl.when(live(which))
            def _():
                fetch(2 * which + 1)
                fetch(2 * which)

    @pl.when(live(slot))
    def _():
        @pl.when(chunk == 0)
        def _():
            arrive(2 * slot)
            arrive(2 * slot + 1)

        left = panels[2 * slot, pl.ds(pl.multiple_of(chunk * CHUNK, CHUNK), CHUNK)]
        product = lax.dot_general(
            left, panels[2 * slot + 1], (((1,), (1,)), ((), ())), preferred_element_type=jnp.float32
        )
        out_ref[0, 0] = product.astype(jnp.bfloat16)

    @pl.when(jnp.logical_not(live(slot)))
    def _():
        out_ref[0, 0] = jnp.zeros((CHUNK, BLOCK), jnp.bfloat16)


def tiles(pairs, panels):
    return pl.pallas_call(
        tile_kernel,
        out_shape=jax.ShapeDtypeStruct((1, 2, BLOCK, BLOCK), jnp.bfloat16),
        grid_spec=pltpu.PrefetchScalarGridSpec(
            num_scalar_prefetch=2,
            grid=(2, BLOCK // CHUNK),
            in_specs=[pl.BlockSpec(memory_space=pl.ANY)],
            out_specs=pl.BlockSpec((1, 1, CHUNK, BLOCK), lambda s, i, *_: (0, s, i, 0)),
            scratch_shapes=[
                pltpu.VMEM((PANELS, BLOCK, SNPS), jnp.bfloat16),
                pltpu.SemaphoreType.DMA((PANELS,)),
            ],
        ),
        name="tile_products",
        compiler_params=pltpu.CompilerParams(vmem_limit_bytes=48 * 2**20),
    )(pairs, jnp.asarray(ITEMS), panels)


def on_device(genotypes, pairs):
    by_panel = pairs.transpose(1, 2, 0).reshape(PANELS, -1)
    return tiles(by_panel, gather(genotypes, by_panel))


def solution(mesh):
    return jax.shard_map(
        on_device,
        mesh=mesh,
        in_specs=(P(("row", "col"), None), P()),
        out_specs=P(("row", "col"), None, None, None),
        check_vma=False,
    )
```

time: 564 us -> 79 us (0.14)
  waiting for transfers between devices: 344 us -> 0 us
  blocking collectives: 131 us -> 0 us
  Pallas kernels: 0 us -> 77.3 us
  local copies, waits for them, and re-layouts: 40.4 us -> 1.37 us
  other arithmetic: 21.5 us -> 0 us
  between operations: 13.4 us -> 0.02 us
  matrix products: 12.9 us -> 0 us
    all_gather x1 -> x0, waiting for transfers between devices: 344 us -> none  [on_device(): everything = lax.all_gather(standard, ('row', 'col'), axis=0, tiled=True)]
    psum x2 -> x0, blocking collectives: 131 us -> none  [the longest x1 68.7 us: on_device(): lax.psum(jnp.sum(counts, axis=0), ('row', 'col')) / sample_total]
    pallas_call x0 -> x2, Pallas kernels: none -> 77.3 us  [the longest x1 64.6 us: gather(): pl.pallas_call(gather_kernel, out_shape=jax.ShapeDtypeStruct((PANELS, STR...]
    gather x3 -> x0, local copies, waits for them, and re-layouts: 39.7 us -> none  [on_device(): panels = jnp.take(all_blocks, wanted_blocks, axis=0)]
    dot_general x2 -> x0, matrix products: 12.9 us -> none  [tile_block(): lax.dot_general(left_panel, right_panel, (((1,), (1,)), ((), ())), prefer...]
    broadcast_in_dim x1 -> x0, other arithmetic: 10.5 us -> none  [on_device(): return jnp.stack([first_tile, second_tile])[None]]
  transfers between devices with their start and end apart: 1 -> 0, of which waited for: 1 -> 0; matrix products, arithmetic and copies ran while one was open for 0% -> 0% of each run, Pallas kernels for 0% -> 0%
where the time goes in v2:
time: 79 us; the launch traced here: 78.7 us
  Pallas kernels  77.3 us (98%)
  local copies, waits for them, and re-layouts  1.37 us (2%)
    pallas_call x1, Pallas kernels, gather(): pl.pallas_call(gather_kernel, out_shape=jax.ShapeDtypeStruct((PANELS, STR...  64.6 us
    pallas_call x1, Pallas kernels, tiles(): pl.pallas_call(tile_kernel, out_shape=jax.ShapeDtypeStruct((1, 2, BLOCK,...  12.7 us

profile of v2, /device:TPU:1, one launch (start us, length us, event | category | flops | bytes accessed | tf_op | source)
XLA Modules:
  0.0 78.7 jit_solution(7602497173954805049)
XLA Ops:
  0.0 64.6 %gather_panels.1.all_ref = bf16[4,2,21,64,512]{4,3,2,1,0:T(8,128)(2,1)} custom-call(s32[256,512]{1,0:T(8,128)} %counts_ref.1, s32[4,128]{1,0:T(4,128)} %bitcast.3, s32[16,21]{1,0:T(8,128)} %constant.4.clone.slots_ref), custom_call_target="tpu_custom_call" | custom-call | tf_op jit(solution)/shard_map/gather_panels/pallas_call | solution.py:336
  64.6 0.0 copy-start
  64.6 0.7 copy-done
  65.3 0.0 copy-start.1
  65.3 0.7 copy-done.1
  66.0 12.7 %tile_products.1 = bf16[1,2,2048,2048]{3,2,1,0:T(8,128)(2,1)} custom-call(s32[4,128]{1,0:T(4,128)S(1)} %bitcast.4, s32[16,21]{1,0:T(8,128)S(1)} %copy-done, bf16[4,2,21,64,512]{4,3,2,1,0:T(8,128)(2,1)} %gather_panels.1.all_ref), custom_call_target="tpu_custom_call" | custom-call | tf_op jit(solution)/shard_map/tile_products/pallas_call | solution.py:428
Async XLA Ops:
  64.6 0.7 copy-start
  65.3 0.7 copy-start.1

commit v3 on v2

v3 whole, which is shorter than its diff:
```python
import jax
import jax.numpy as jnp
import numpy as np
from jax import lax
from jax.experimental import pallas as pl
from jax.experimental.pallas import tpu as pltpu
from jax.sharding import PartitionSpec as P

MESH = pl.DeviceIdType.MESH
SNPS = 512
RING = 4
ROW_COUNT = 16
COL_COUNT = 8
SHARD = 256
SAMPLES = SHARD * ROW_COUNT * COL_COUNT
BLOCK = SHARD * COL_COUNT
STREAMS = 2
PARTS = 2
PIECE = SHARD // (STREAMS * PARTS)
PANELS = 4
LINKS = ((1, 0, 0), (3, 0, 0), (0, 1, 0), (0, 3, 0), (0, 0, 1), (0, 0, 3))
PER_LINK = 2
CHUNK = 512

RELAYS = (
    ((0, 16), (0, 48), (1, 4), (1, 12), (1, 1), (0, 3)),
    ((0, 32), (1, 48), (0, 4), (0, 60), (1, 2), (0, 19)),
    ((1, 17), (1, 52), (0, 20), (0, 15), (1, 13), (1, 15)),
    ((1, 31), (1, 36), (0, 24), (1, 9), (0, 61), (0, 23)),
    ((0, 39), (0, 63), (1, 6), (0, 44), (0, 25), (1, 55)),
    ((1, 47), (0, 45), (0, 49), (1, 27), (1, 37), (0, 22)),
    ((0, 38), (0, 6), (1, 59), (0, 59), (0, 46), (1, 46)),
)
DIRECT = (
    ((0, 1), (0, 13), (0, 40), (0, 41), (0, 54), (0, 62), (1, 11), (1, 18), (1, 22), (1, 25), (1, 29), (1, 33), (1, 53), (1, 62)),
    ((0, 8), (0, 9), (0, 30), (0, 33), (0, 43), (1, 20), (1, 21), (1, 30), (1, 32), (1, 43), (1, 50), (1, 54), (1, 57), (1, 61)),
    ((0, 10), (0, 26), (0, 29), (0, 52), (0, 53), (1, 3), (1, 10), (1, 19), (1, 34), (1, 35), (1, 40), (1, 41), (1, 63)),
    ((0, 2), (0, 11), (0, 28), (0, 31), (0, 34), (0, 35), (0, 42), (0, 55), (0, 57), (1, 8), (1, 23), (1, 42), (1, 51), (1, 60)),
    ((0, 5), (0, 12), (0, 17), (0, 21), (0, 36), (0, 50), (0, 56), (1, 5), (1, 14), (1, 24), (1, 28), (1, 38), (1, 44), (1, 49), (1, 56)),
    ((0, 7), (0, 14), (0, 18), (0, 27), (0, 37), (0, 47), (0, 51), (0, 58), (1, 7), (1, 16), (1, 26), (1, 39), (1, 45), (1, 58)),
)

def offset_of(n):
    return n // (RING * RING), n // RING % RING, n % RING


def number(offset):
    return (offset[0] * RING + offset[1]) * RING + offset[2]


def before(n, link):
    return number(tuple((i - j) % RING for i, j in zip(offset_of(n), LINKS[link])))


HELD = tuple((p, 0) for p in range(PARTS)) + tuple(item for step in RELAYS for item in step)
LANES = 128
SLOT_OF = {item: i for i, item in enumerate(HELD)}
CAME_BY = {item: link for step in RELAYS for link, item in enumerate(step)}


def class_of(n, y_lo):
    dx, dy, _ = offset_of(n)
    return (dx * 2 + y_lo) * 2 + ((dy + 1 - y_lo) // 2) % 2


def tables():
    table = np.zeros((18, LANES), np.int32)
    own_most = 0
    for y_lo in range(2):
        for kind in sorted({class_of(n, y_lo) for n in range(RING**3)}):
            places = []
            for e, items in enumerate(DIRECT):
                mine = [(p, n) for p, n in items if class_of(n, y_lo) == kind]
                assert len(mine) <= PER_LINK
                places += [(e * PER_LINK + i, SLOT_OF[p, before(n, e)], p, n) for i, (p, n) in enumerate(mine)]
            own = [(slot, p, n) for slot, (p, n) in enumerate(HELD) if class_of(n, y_lo) == kind]
            own_most = max(own_most, len(own))
            places += [(FROM_LINKS + i, *one) for i, one in enumerate(own)]
            assert len(places) == PARTS * COL_COUNT
            for place, slot, p, n in places:
                table[kind, place] = slot
                table[16 + y_lo, p * RING**3 + n] = place
    return table, own_most


FROM_LINKS = len(LINKS) * PER_LINK
TABLE, OWN = tables()
PIECES = FROM_LINKS + OWN


def place_of_self():
    row, col = lax.axis_index("row"), lax.axis_index("col")
    return (row // 2) % RING, (row // 8) * 2 + col // RING, col % RING, row % 2


def kind_of(block, x, y):
    behind = (x - lax.shift_right_logical(block, 1)) & (RING - 1)
    half = ((y // 2) - lax.shift_right_logical(block, 3)) & 1
    return (behind * 2 + y % 2) * 2 + half


def gather_kernel(
    counts_hbm, pairs_hbm, table_hbm, tile_ref, panels_ref,
    counts_ref, pairs_ref, table_ref, held, sums, away, near, landed0, landed1, landed2, landed3, left, right,
    load_sem, twin_send, twin_recv, relay_send, relay_recv, stat_send, stat_recv,
    link_send, link_recv, near_send, near_recv,
):
    x, y, z, core = place_of_self()
    landed = (landed0, landed1, landed2, landed3)

    def place(offset):
        return tuple((me + step) % RING for me, step in zip((x, y, z), offset))

    def device_at(offset, on_core):
        px, py, pz = place(offset)
        return ((py // 2) * RING + px) * 2 + on_core, (py % 2) * RING + pz

    here = (0, 0, 0)
    twin = device_at(here, 1 - core)
    neighbours = [device_at(link, core) for link in LINKS]
    across = [device_at(tuple(2 * (a == axis) for a in range(3)), core) for axis in range(3)]
    others = [device_at(link, 1 - core) for link in LINKS]

    barrier = pltpu.get_barrier_semaphore()
    peers = [twin, *neighbours, *others, *across]
    for peer in peers:
        pl.semaphore_signal(barrier, inc=1, device_id=peer, device_id_type=MESH)
    loads = [
        pltpu.make_async_copy(source, target, load_sem.at[i])
        for i, (source, target) in enumerate(
            ((counts_hbm, counts_ref), (pairs_hbm, pairs_ref), (table_hbm, table_ref))
        )
    ]
    for load in loads:
        load.start()
    loads[0].wait()

    def as_bf16(first, rows):
        return counts_ref[pl.ds(first, rows)].astype(jnp.float32).astype(jnp.bfloat16)

    mine, theirs = core * (SHARD // 2), (1 - core) * (SHARD // 2)
    for p in range(PARTS):
        near[2, p] = as_bf16(pl.multiple_of(theirs + p * PIECE, PIECE), PIECE)
        held[p, core] = as_bf16(pl.multiple_of(mine + p * PIECE, PIECE), PIECE)
    halves = (core, 1 - core)

    def swap(p, half):
        return pltpu.make_async_remote_copy(
            src_ref=near.at[2, p],
            dst_ref=held.at[p, half],
            send_sem=twin_send.at[p],
            recv_sem=twin_recv.at[p],
            device_id=twin,
            device_id_type=MESH,
        )

    pl.semaphore_wait(barrier, len(peers))
    for p in range(PARTS):
        swap(p, core).start()

    def sum_to(slot, source, target):
        return pltpu.make_async_remote_copy(
            src_ref=sums.at[source],
            dst_ref=sums.at[slot],
            send_sem=stat_send.at[slot],
            recv_sem=stat_recv.at[slot],
            device_id=target,
            device_id_type=MESH,
        )

    def stat_copies(phase):
        if phase == 0:
            return [sum_to(1, 0, twin)]
        axis, base = phase - 1, 4 * phase - 2
        targets = [neighbours[2 * axis], neighbours[2 * axis + 1], across[axis]]
        return [sum_to(base + 1 + i, base, target) for i, target in enumerate(targets)]

    def stat_finish(phase):
        for copy in stat_copies(phase):
            copy.wait()
        if phase == 0:
            sums[2] = sums[0] + sums[1]
        else:
            base = 4 * phase - 2
            sums[base + 4] = (sums[base] + sums[base + 1]) + (sums[base + 2] + sums[base + 3])

    def stat_start():
        counts = counts_ref[...]
        total = jnp.sum(counts, axis=0, keepdims=True)
        square = jnp.sum(counts * counts, axis=0, keepdims=True)
        which = lax.broadcasted_iota(jnp.int32, (8, SNPS), 0)
        sums[0] = jnp.where(which == 0, total, jnp.where(which == 1, square, 0))
        for copy in stat_copies(0):
            copy.start()

    def relay(item, half):
        slot, link = SLOT_OF[item], CAME_BY[item]
        source = SLOT_OF[item[0], before(item[1], link)]
        return pltpu.make_async_remote_copy(
            src_ref=held.at[source, halves[half]],
            dst_ref=held.at[slot, halves[half]],
            send_sem=relay_send.at[slot, half],
            recv_sem=relay_recv.at[slot, half],
            device_id=neighbours[link],
            device_id_type=MESH,
        )

    arrived = {((p, 0), 0) for p in range(PARTS)}

    def arrive(item, half):
        if (item, half) not in arrived:
            arrived.add((item, half))
            if item[1] == 0:
                swap(item[0], halves[1]).wait_recv()
            else:
                relay(item, half).wait_recv()

    for t, step in enumerate(RELAYS):
        for half in range(2):
            for link, item in enumerate(step):
                arrive((item[0], before(item[1], link)), half)
                relay(item, half).start()
            if t == 0 and half == 0:
                stat_start()
        if 0 < t < 5:
            stat_finish(t - 1)
            if t < 4:
                for copy in stat_copies(t):
                    copy.start()
    for step in RELAYS:
        for half in range(2):
            for item in step:
                arrive(item, half)
    loads[1].wait()
    loads[2].wait()

    total, square = sums[14, 0:1], sums[14, 1:2]
    shifted = total - SAMPLES
    spread = SAMPLES * (square - 2 * total + SAMPLES) - shifted * shifted
    variance = spread.astype(jnp.float32) * (1.0 / (float(SAMPLES) * SAMPLES)) + 1e-05
    mean = total.astype(jnp.float32) * (1.0 / SAMPLES)
    scale = lax.rsqrt(variance)

    def standard(slot, half, factor):
        return ((held[slot, half].astype(jnp.float32) - mean) * (scale * factor)).astype(jnp.bfloat16)

    def wanted(device, panel):
        return jnp.maximum(pairs_ref[panel, device[0] * COL_COUNT + device[1]], 0)

    def step_of(link):
        step = 1 + 2 * (link % 2)
        return tuple(jnp.where(link // 2 == axis, step, 0) for axis in range(3))

    def to_link(link, to_core, panel, stream):
        return pltpu.make_async_remote_copy(
            src_ref=away.at[link, to_core, panel % 2],
            dst_ref=landed[panel].at[stream, pl.ds(link * PER_LINK, PER_LINK)],
            send_sem=link_send.at[link, to_core, panel],
            recv_sem=link_recv.at[link, stream, panel],
            device_id=device_at(step_of(link), to_core),
            device_id_type=MESH,
        )

    def to_twin(panel, stream):
        return pltpu.make_async_remote_copy(
            src_ref=near.at[panel % 2],
            dst_ref=landed[panel].at[stream, pl.ds(FROM_LINKS, OWN)],
            send_sem=near_send.at[panel],
            recv_sem=near_recv.at[panel],
            device_id=twin,
            device_id_type=MESH,
        )

    def sent(panel):
        for link in range(len(LINKS)):
            for to_core in range(2):
                to_link(link, to_core, panel, core).wait_send()
        to_twin(panel, core).wait_send()

    def send_panel(panel):
        if panel >= 2:
            sent(panel - 2)
        factor = 1.0 / SNPS if panel % 2 == 0 else 1.0

        def message(m, carry):
            to_core, link = m // len(LINKS), m % len(LINKS)
            step = step_of(link)
            block = wanted(device_at(step, to_core), panel)
            px, py, _ = place(step)
            kind = kind_of(block, px, py)
            for i in range(PER_LINK):
                slot = table_ref[kind, link * PER_LINK + i]
                away[link, to_core, panel % 2, i] = standard(slot, block & 1, factor)
            to_link(link, to_core, panel, core).start()
            return carry

        lax.fori_loop(0, 2 * len(LINKS), message, 0)
        for device in (twin, device_at(here, core)):
            block = wanted(device, panel)
            kind = kind_of(block, x, y)

            def one(i, carry):
                piece = standard(table_ref[kind, FROM_LINKS + i], block & 1, factor)
                if device is twin:
                    near[panel % 2, i] = piece
                else:
                    landed[panel][core, FROM_LINKS + i] = piece
                return carry

            lax.fori_loop(0, OWN, one, 0)
            if device is twin:
                to_twin(panel, core).start()

    for panel in range(PANELS):
        send_panel(panel)

    def in_order(panel, target):
        for link in range(len(LINKS)):
            for stream in range(STREAMS):
                to_link(link, 0, panel, stream).wait_recv()
        to_twin(panel, 1 - core).wait_recv()
        block = wanted(device_at(here, core), panel)
        live = pairs_ref[panel, device_at(here, core)[0] * COL_COUNT + device_at(here, core)[1]] >= 0
        keep = jnp.where(live, 1.0, 0.0).astype(jnp.bfloat16)
        dx = (x - lax.shift_right_logical(block, 1)) & (RING - 1)

        def one(col, carry):
            dy = (y - (2 * lax.shift_right_logical(block, 3) + col // RING)) & (RING - 1)
            dz = (z - col % RING) & (RING - 1)
            for p in range(PARTS):
                place = table_ref[16 + y % 2, p * RING**3 + (dx * RING + dy) * RING + dz]
                for stream in range(STREAMS):
                    first = col * SHARD + stream * (SHARD // 2) + p * PIECE
                    rows = pl.ds(pl.multiple_of(first, PIECE), PIECE)
                    target[rows] = landed[panel][stream, place] * keep
            return carry

        lax.fori_loop(0, COL_COUNT, one, 0)

    in_order(0, left)
    in_order(1, right)

    def multiply(i, carry):
        rows = pl.ds(pl.multiple_of(i * CHUNK, CHUNK), CHUNK)
        product = lax.dot_general(
            left[rows], right[...], (((1,), (1,)), ((), ())), preferred_element_type=jnp.float32
        )
        tile_ref[rows] = product.astype(jnp.bfloat16)
        return carry

    lax.fori_loop(0, BLOCK // CHUNK, multiply, 0)
    in_order(2, panels_ref.at[0])
    in_order(3, panels_ref.at[1])
    for panel in (2, 3):
        sent(panel)
    for p in range(PARTS):
        swap(p, core).wait_send()
    for step in RELAYS:
        for half in range(2):
            for item in step:
                relay(item, half).wait_send()


def gather(counts, pairs):
    dma = pltpu.SemaphoreType.DMA
    bf16 = jnp.bfloat16
    return pl.pallas_call(
        gather_kernel,
        out_shape=(
            jax.ShapeDtypeStruct((BLOCK, BLOCK), bf16),
            jax.ShapeDtypeStruct((2, BLOCK, SNPS), bf16),
        ),
        in_specs=[pl.BlockSpec(memory_space=pltpu.HBM)] * 3,
        out_specs=(pl.BlockSpec(memory_space=pltpu.VMEM),) * 2,
        scratch_shapes=[
            pltpu.VMEM((SHARD, SNPS), jnp.int32),
            pltpu.SMEM((PANELS, LANES), jnp.int32),
            pltpu.SMEM(TABLE.shape, jnp.int32),
            pltpu.VMEM((len(HELD), 2, PIECE, SNPS), bf16),
            pltpu.VMEM((15, 8, SNPS), jnp.int32),
            pltpu.VMEM((len(LINKS), 2, 2, PER_LINK, PIECE, SNPS), bf16),
            pltpu.VMEM((3, OWN, PIECE, SNPS), bf16),
            *[pltpu.VMEM((STREAMS, PIECES, PIECE, SNPS), bf16) for _ in range(PANELS)],
            pltpu.VMEM((BLOCK, SNPS), bf16),
            pltpu.VMEM((BLOCK, SNPS), bf16),
            dma((3,)),
            dma((PARTS,)),
            dma((PARTS,)),
            dma((len(HELD), 2)),
            dma((len(HELD), 2)),
            dma((15,)),
            dma((15,)),
            dma((len(LINKS), 2, PANELS)),
            dma((len(LINKS), 2, PANELS)),
            dma((PANELS,)),
            dma((PANELS,)),
        ],
        name="gather_panels",
        compiler_params=pltpu.CompilerParams(
            collective_id=0, has_side_effects=True, vmem_limit_bytes=36 * 2**20
        ),
    )(*(pltpu.with_memory_space_constraint(a, pltpu.HBM) for a in (counts, pairs, jnp.asarray(TABLE))))


def tile_kernel(tile_ref, panels_ref, out_ref, buffer, sem):
    first = pltpu.make_async_copy(tile_ref, out_ref.at[0, 0], sem.at[0])
    first.start()
    count = BLOCK // CHUNK

    def write(i):
        rows = pl.ds(i * CHUNK, CHUNK)
        return pltpu.make_async_copy(buffer.at[rows], out_ref.at[0, 1, rows], sem.at[1 + i])

    for i in range(count):
        rows = pl.ds(i * CHUNK, CHUNK)
        product = lax.dot_general(
            panels_ref[0, rows], panels_ref[1], (((1,), (1,)), ((), ())), preferred_element_type=jnp.float32
        )
        buffer[rows] = product.astype(jnp.bfloat16)
        write(i).start()
    first.wait()
    for i in range(count):
        write(i).wait()


def tiles(tile, panels):
    return pl.pallas_call(
        tile_kernel,
        out_shape=jax.ShapeDtypeStruct((1, 2, BLOCK, BLOCK), jnp.bfloat16),
        in_specs=[pl.BlockSpec(memory_space=pl.ANY), pl.BlockSpec(memory_space=pltpu.VMEM)],
        out_specs=pl.BlockSpec(memory_space=pl.ANY),
        scratch_shapes=[
            pltpu.VMEM((BLOCK, BLOCK), jnp.bfloat16),
            pltpu.SemaphoreType.DMA((1 + BLOCK // CHUNK,)),
        ],
        name="tile_products",
        compiler_params=pltpu.CompilerParams(vmem_limit_bytes=24 * 2**20),
    )(tile, panels)


def on_device(genotypes, pairs):
    by_panel = pairs.transpose(1, 2, 0).reshape(PANELS, -1)
    return tiles(*gather(genotypes, by_panel))


def solution(mesh):
    return jax.shard_map(
        on_device,
        mesh=mesh,
        in_specs=(P(("row", "col"), None), P()),
        out_specs=P(("row", "col"), None, None, None),
        check_vma=False,
    )
```

time: 79 us -> 67.4 us (0.85)
  Pallas kernels: 77.3 us -> 67.2 us
  local copies, waits for them, and re-layouts: 1.37 us -> 0 us
    pallas_call x1, Pallas kernels: 12.7 us -> 6.02 us  [tiles(): pl.pallas_call(tile_kernel, out_shape=jax.ShapeDtypeStruct((1, 2, BLOCK,...]
    pallas_call x1, Pallas kernels: 64.6 us -> 61.2 us  [gather(): pl.pallas_call(gather_kernel, out_shape=(jax.ShapeDtypeStruct((BLOCK, BLO...]
    unnamed x4 -> x0, local copies, waits for them, and re-layouts: 1.37 us -> none
where the time goes in v3:
time: 67.4 us; the launch traced here: 67.3 us
  Pallas kernels  67.2 us (100%)
    pallas_call x1, Pallas kernels, gather(): pl.pallas_call(gather_kernel, out_shape=(jax.ShapeDtypeStruct((BLOCK, BLO...  61.2 us
    pallas_call x1, Pallas kernels, tiles(): pl.pallas_call(tile_kernel, out_shape=jax.ShapeDtypeStruct((1, 2, BLOCK,...  6.02 us

profile of v3, /device:TPU:1, one launch (start us, length us, event | category | flops | bytes accessed | tf_op | source)
XLA Modules:
  0.0 67.3 jit_solution(595577506140790284)
XLA Ops:
  0.0 61.2 %gather_panels.1 = (bf16[2048,2048]{1,0:T(8,128)(2,1)S(1)}, bf16[2,2048,512]{2,1,0:T(8,128)(2,1)S(1)}) custom-call(s32[256,512]{1,0:T(8,128)} %counts_hbm.1, s32[4,128]{1,0:T(4,128)} %bitcast.3, s32[18,128]{1,0:T(8,128)} %constant.2.clone.table_hbm), custom_call_target="tpu_custom_call" | custom-call | tf_op jit(solution)/shard_map/gather_panels/pallas_call | solution.py:367
  61.2 6.0 %tile_products.1 = bf16[1,2,2048,2048]{3,2,1,0:T(8,128)(2,1)} custom-call(bf16[2048,2048]{1,0:T(8,128)(2,1)S(1)} %get-tuple-element.7.tile_ref, bf16[2,2048,512]{2,1,0:T(8,128)(2,1)S(1)} %get-tuple-element.8.panels_ref), custom_call_target="tpu_custom_call" | custom-call | tf_op jit(solution)/shard_map/tile_products/pallas_call | solution.py:427

commit v4 on v3

--- a/solution.py
+++ b/solution.py
@@ -23,22 +23,22 @@
 CHUNK = 512
 
 RELAYS = (
-    ((0, 16), (0, 48), (1, 4), (1, 12), (1, 1), (0, 3)),
-    ((0, 32), (1, 48), (0, 4), (0, 60), (1, 2), (0, 19)),
-    ((1, 17), (1, 52), (0, 20), (0, 15), (1, 13), (1, 15)),
-    ((1, 31), (1, 36), (0, 24), (1, 9), (0, 61), (0, 23)),
-    ((0, 39), (0, 63), (1, 6), (0, 44), (0, 25), (1, 55)),
-    ((1, 47), (0, 45), (0, 49), (1, 27), (1, 37), (0, 22)),
-    ((0, 38), (0, 6), (1, 59), (0, 59), (0, 46), (1, 46)),
+    ((1, 16), (0, 48), (0, 4), (1, 12), (1, 1), (0, 3)),
+    ((0, 20), (1, 60), (0, 52), (1, 28), (0, 49), (1, 19)),
+    ((0, 36), (1, 44), (1, 5), (0, 15), (0, 21), (1, 63)),
+    ((1, 35), (0, 33), (0, 24), (1, 56), (1, 29), (0, 55)),
+    ((0, 40), (1, 40), (0, 25), (1, 59), (0, 34), (1, 34)),
+    ((1, 11), (0, 9), (1, 38), (0, 46), (1, 30), (0, 54)),
 )
 DIRECT = (
-    ((0, 1), (0, 13), (0, 40), (0, 41), (0, 54), (0, 62), (1, 11), (1, 18), (1, 22), (1, 25), (1, 29), (1, 33), (1, 53), (1, 62)),
-    ((0, 8), (0, 9), (0, 30), (0, 33), (0, 43), (1, 20), (1, 21), (1, 30), (1, 32), (1, 43), (1, 50), (1, 54), (1, 57), (1, 61)),
-    ((0, 10), (0, 26), (0, 29), (0, 52), (0, 53), (1, 3), (1, 10), (1, 19), (1, 34), (1, 35), (1, 40), (1, 41), (1, 63)),
-    ((0, 2), (0, 11), (0, 28), (0, 31), (0, 34), (0, 35), (0, 42), (0, 55), (0, 57), (1, 8), (1, 23), (1, 42), (1, 51), (1, 60)),
-    ((0, 5), (0, 12), (0, 17), (0, 21), (0, 36), (0, 50), (0, 56), (1, 5), (1, 14), (1, 24), (1, 28), (1, 38), (1, 44), (1, 49), (1, 56)),
-    ((0, 7), (0, 14), (0, 18), (0, 27), (0, 37), (0, 47), (0, 51), (0, 58), (1, 7), (1, 16), (1, 26), (1, 39), (1, 45), (1, 58)),
+    ((0, 1), (0, 6), (0, 19), (0, 31), (0, 37), (0, 41), (0, 56), (0, 62), (1, 8), (1, 15), (1, 21), (1, 27), (1, 32), (1, 45), (1, 50), (1, 54)),
+    ((0, 5), (0, 8), (0, 18), (0, 30), (0, 32), (0, 39), (0, 57), (0, 63), (1, 3), (1, 14), (1, 22), (1, 24), (1, 43), (1, 47), (1, 49), (1, 53)),
+    ((0, 13), (0, 28), (0, 29), (0, 38), (0, 44), (0, 58), (0, 59), (1, 4), (1, 9), (1, 20), (1, 23), (1, 42), (1, 48), (1, 51)),
+    ((0, 11), (0, 12), (0, 16), (0, 17), (0, 42), (0, 60), (0, 61), (1, 7), (1, 25), (1, 26), (1, 36), (1, 46), (1, 52), (1, 55)),
+    ((0, 10), (0, 22), (0, 26), (0, 35), (0, 47), (0, 50), (0, 53), (1, 2), (1, 6), (1, 13), (1, 17), (1, 39), (1, 41), (1, 57), (1, 61)),
+    ((0, 2), (0, 7), (0, 14), (0, 23), (0, 27), (0, 43), (0, 45), (0, 51), (1, 10), (1, 18), (1, 31), (1, 33), (1, 37), (1, 58), (1, 62)),
 )
+
 
 def offset_of(n):
     return n // (RING * RING), n // RING % RING, n % RING
@@ -125,23 +125,25 @@
     peers = [twin, *neighbours, *others, *across]
     for peer in peers:
         pl.semaphore_signal(barrier, inc=1, device_id=peer, device_id_type=MESH)
+
+    mine, theirs = core * (SHARD // 2), (1 - core) * (SHARD // 2)
+    quarters = [pl.ds(pl.multiple_of(half + p * PIECE, PIECE), PIECE) for half in (theirs, mine) for p in range(PARTS)]
     loads = [
         pltpu.make_async_copy(source, target, load_sem.at[i])
         for i, (source, target) in enumerate(
-            ((counts_hbm, counts_ref), (pairs_hbm, pairs_ref), (table_hbm, table_ref))
+            [(counts_hbm.at[rows], counts_ref.at[rows]) for rows in quarters]
+            + [(pairs_hbm, pairs_ref), (table_hbm, table_ref)]
         )
     ]
     for load in loads:
         load.start()
-    loads[0].wait()
-
-    def as_bf16(first, rows):
-        return counts_ref[pl.ds(first, rows)].astype(jnp.float32).astype(jnp.bfloat16)
-
-    mine, theirs = core * (SHARD // 2), (1 - core) * (SHARD // 2)
-    for p in range(PARTS):
-        near[2, p] = as_bf16(pl.multiple_of(theirs + p * PIECE, PIECE), PIECE)
-        held[p, core] = as_bf16(pl.multiple_of(mine + p * PIECE, PIECE), PIECE)
+    for i, rows in enumerate(quarters):
+        loads[i].wait()
+        quarter = counts_ref[rows].astype(jnp.float32).astype(jnp.bfloat16)
+        if i < PARTS:
+            near[2, i] = quarter
+        else:
+            held[i - PARTS, core] = quarter
     halves = (core, 1 - core)
 
     def swap(p, half):
@@ -231,8 +233,8 @@
         for half in range(2):
             for item in step:
                 arrive(item, half)
-    loads[1].wait()
-    loads[2].wait()
+    loads[4].wait()
+    loads[5].wait()
 
     total, square = sums[14, 0:1], sums[14, 1:2]
     shifted = total - SAMPLES
@@ -332,33 +334,34 @@
                 for stream in range(STREAMS):
                     first = col * SHARD + stream * (SHARD // 2) + p * PIECE
                     rows = pl.ds(pl.multiple_of(first, PIECE), PIECE)
-                    target[rows] = landed[panel][stream, place] * keep
+                    piece = landed[panel][stream, place]
+                    target[rows] = piece * keep if panel % 2 == 0 else piece
             return carry
 
         lax.fori_loop(0, COL_COUNT, one, 0)
 
-    in_order(0, left)
-    in_order(1, right)
-
-    def multiply(i, carry):
-        rows = pl.ds(pl.multiple_of(i * CHUNK, CHUNK), CHUNK)
-        product = lax.dot_general(
-            left[rows], right[...], (((1,), (1,)), ((), ())), preferred_element_type=jnp.float32
-        )
-        tile_ref[rows] = product.astype(jnp.bfloat16)
-        return carry
-
-    lax.fori_loop(0, BLOCK // CHUNK, multiply, 0)
-    in_order(2, panels_ref.at[0])
-    in_order(3, panels_ref.at[1])
-    for panel in (2, 3):
-        sent(panel)
     for p in range(PARTS):
         swap(p, core).wait_send()
     for step in RELAYS:
         for half in range(2):
             for item in step:
                 relay(item, half).wait_send()
+    in_order(0, left)
+    in_order(1, right)
+
+    def multiply(i, carry):
+        rows = pl.ds(pl.multiple_of(i * CHUNK, CHUNK), CHUNK)
+        product = lax.dot_general(
+            left[rows], right[...], (((1,), (1,)), ((), ())), preferred_element_type=jnp.float32
+        )
+        tile_ref[rows] = product.astype(jnp.bfloat16)
+        return carry
+
+    lax.fori_loop(0, BLOCK // CHUNK, multiply, 0)
+    in_order(2, panels_ref.at[0])
+    in_order(3, panels_ref.at[1])
+    for panel in (2, 3):
+        sent(panel)
 
 
 def gather(counts, pairs):
@@ -383,7 +386,7 @@
             *[pltpu.VMEM((STREAMS, PIECES, PIECE, SNPS), bf16) for _ in range(PANELS)],
             pltpu.VMEM((BLOCK, SNPS), bf16),
             pltpu.VMEM((BLOCK, SNPS), bf16),
-            dma((3,)),
+            dma((6,)),
             dma((PARTS,)),
             dma((PARTS,)),
             dma((len(HELD), 2)),

time: 67.4 us -> 64.7 us (0.960)
  Pallas kernels: 67.2 us -> 64.6 us
    pallas_call x1, Pallas kernels: 61.2 us -> 58.6 us  [gather(): pl.pallas_call(gather_kernel, out_shape=(jax.ShapeDtypeStruct((BLOCK, BLO...]
where the time goes in v4:
time: 64.7 us; the launch traced here: 64.6 us
  Pallas kernels  64.6 us (100%)
    pallas_call x1, Pallas kernels, gather(): pl.pallas_call(gather_kernel, out_shape=(jax.ShapeDtypeStruct((BLOCK, BLO...  58.6 us
    pallas_call x1, Pallas kernels, tiles(): pl.pallas_call(tile_kernel, out_shape=jax.ShapeDtypeStruct((1, 2, BLOCK,...  6.02 us

profile of v4, /device:TPU:1, one launch (start us, length us, event | category | flops | bytes accessed | tf_op | source)
XLA Modules:
  0.0 64.6 jit_solution(9559164093976439649)
XLA Ops:
  0.0 58.6 %gather_panels.1 = (bf16[2048,2048]{1,0:T(8,128)(2,1)S(1)}, bf16[2,2048,512]{2,1,0:T(8,128)(2,1)S(1)}) custom-call(s32[256,512]{1,0:T(8,128)} %counts_hbm.1, s32[4,128]{1,0:T(4,128)} %bitcast.3, s32[18,128]{1,0:T(8,128)} %constant.2.clone.table_hbm), custom_call_target="tpu_custom_call" | custom-call | tf_op jit(solution)/shard_map/gather_panels/pallas_call | solution.py:370
  58.6 6.0 %tile_products.1 = bf16[1,2,2048,2048]{3,2,1,0:T(8,128)(2,1)} custom-call(bf16[2048,2048]{1,0:T(8,128)(2,1)S(1)} %get-tuple-element.7.tile_ref, bf16[2,2048,512]{2,1,0:T(8,128)(2,1)S(1)} %get-tuple-element.8.panels_ref), custom_call_target="tpu_custom_call" | custom-call | tf_op jit(solution)/shard_map/tile_products/pallas_call | solution.py:430

commit v5 on v4

--- a/solution.py
+++ b/solution.py
@@ -37,6 +37,13 @@
     ((0, 11), (0, 12), (0, 16), (0, 17), (0, 42), (0, 60), (0, 61), (1, 7), (1, 25), (1, 26), (1, 36), (1, 46), (1, 52), (1, 55)),
     ((0, 10), (0, 22), (0, 26), (0, 35), (0, 47), (0, 50), (0, 53), (1, 2), (1, 6), (1, 13), (1, 17), (1, 39), (1, 41), (1, 57), (1, 61)),
     ((0, 2), (0, 7), (0, 14), (0, 23), (0, 27), (0, 43), (0, 45), (0, 51), (1, 10), (1, 18), (1, 31), (1, 33), (1, 37), (1, 58), (1, 62)),
+)
+
+ORDER = (
+    0, 2, 4, 6, 8, 10, 1, 3, 5, 7, 9, 11, 18, 22, 16, 20, 12, 14,
+    19, 23, 17, 21, 13, 15, 30, 29, 44, 36, 46, 38, 42, 40, 32, 37, 34, 39,
+    43, 41, 33, 25, 35, 27, 31, 28, 45, 24, 58, 50, 52, 54, 57, 48, 59, 51,
+    53, 55, 56, 49, 47, 26, 64, 69, 70, 62, 60, 67, 65, 68, 63, 61, 66, 71,
 )
 
 
@@ -217,14 +224,14 @@
             else:
                 relay(item, half).wait_recv()
 
-    for t, step in enumerate(RELAYS):
-        for half in range(2):
-            for link, item in enumerate(step):
-                arrive((item[0], before(item[1], link)), half)
-                relay(item, half).start()
-            if t == 0 and half == 0:
-                stat_start()
-        if 0 < t < 5:
+    for i, code in enumerate(ORDER):
+        item, half = HELD[PARTS + code // 2], code % 2
+        arrive((item[0], before(item[1], CAME_BY[item])), half)
+        relay(item, half).start()
+        if i == len(LINKS) - 1:
+            stat_start()
+        t, last = divmod(i, 2 * len(LINKS))
+        if last == 2 * len(LINKS) - 1 and 0 < t < 5:
             stat_finish(t - 1)
             if t < 4:
                 for copy in stat_copies(t):

time: 64.7 us -> 63 us (0.974)
  Pallas kernels: 64.6 us -> 62.8 us
    pallas_call x1, Pallas kernels: 58.6 us -> 56.8 us  [gather(): pl.pallas_call(gather_kernel, out_shape=(jax.ShapeDtypeStruct((BLOCK, BLO...]
where the time goes in v5:
time: 63 us; the launch traced here: 62.9 us
  Pallas kernels  62.8 us (100%)
    pallas_call x1, Pallas kernels, gather(): pl.pallas_call(gather_kernel, out_shape=(jax.ShapeDtypeStruct((BLOCK, BLO...  56.8 us
    pallas_call x1, Pallas kernels, tiles(): pl.pallas_call(tile_kernel, out_shape=jax.ShapeDtypeStruct((1, 2, BLOCK,...  6.02 us

profile of v5, /device:TPU:1, one launch (start us, length us, event | category | flops | bytes accessed | tf_op | source)
XLA Modules:
  0.0 62.9 jit_solution(2792779954297884033)
XLA Ops:
  0.0 56.8 %gather_panels.1 = (bf16[2048,2048]{1,0:T(8,128)(2,1)S(1)}, bf16[2,2048,512]{2,1,0:T(8,128)(2,1)S(1)}) custom-call(s32[256,512]{1,0:T(8,128)} %counts_hbm.1, s32[4,128]{1,0:T(4,128)} %bitcast.3, s32[18,128]{1,0:T(8,128)} %constant.2.clone.table_hbm), custom_call_target="tpu_custom_call" | custom-call | tf_op jit(solution)/shard_map/gather_panels/pallas_call | solution.py:377
  56.8 6.0 %tile_products.1 = bf16[1,2,2048,2048]{3,2,1,0:T(8,128)(2,1)} custom-call(bf16[2048,2048]{1,0:T(8,128)(2,1)S(1)} %get-tuple-element.7.tile_ref, bf16[2,2048,512]{2,1,0:T(8,128)(2,1)S(1)} %get-tuple-element.8.panels_ref), custom_call_target="tpu_custom_call" | custom-call | tf_op jit(solution)/shard_map/tile_products/pallas_call | solution.py:437

commit v6 on v5

--- a/solution.py
+++ b/solution.py
@@ -21,6 +21,7 @@
 LINKS = ((1, 0, 0), (3, 0, 0), (0, 1, 0), (0, 3, 0), (0, 0, 1), (0, 0, 3))
 PER_LINK = 2
 CHUNK = 512
+STAT_AFTER = (20, 38, 54, 71)
 
 RELAYS = (
     ((1, 16), (0, 48), (0, 4), (1, 12), (1, 1), (0, 3)),
@@ -130,8 +131,6 @@
 
     barrier = pltpu.get_barrier_semaphore()
     peers = [twin, *neighbours, *others, *across]
-    for peer in peers:
-        pl.semaphore_signal(barrier, inc=1, device_id=peer, device_id_type=MESH)
 
     mine, theirs = core * (SHARD // 2), (1 - core) * (SHARD // 2)
     quarters = [pl.ds(pl.multiple_of(half + p * PIECE, PIECE), PIECE) for half in (theirs, mine) for p in range(PARTS)]
@@ -144,6 +143,8 @@
     ]
     for load in loads:
         load.start()
+    for peer in peers:
+        pl.semaphore_signal(barrier, inc=1, device_id=peer, device_id_type=MESH)
     for i, rows in enumerate(quarters):
         loads[i].wait()
         quarter = counts_ref[rows].astype(jnp.float32).astype(jnp.bfloat16)
@@ -230,8 +231,8 @@
         relay(item, half).start()
         if i == len(LINKS) - 1:
             stat_start()
-        t, last = divmod(i, 2 * len(LINKS))
-        if last == 2 * len(LINKS) - 1 and 0 < t < 5:
+        if i in STAT_AFTER:
+            t = STAT_AFTER.index(i) + 1
             stat_finish(t - 1)
             if t < 4:
                 for copy in stat_copies(t):

time: 63 us -> 63.6 us (level)
  Pallas kernels: 62.8 us -> 63.5 us
    pallas_call x1, Pallas kernels: 56.8 us -> 57.5 us  [gather(): pl.pallas_call(gather_kernel, out_shape=(jax.ShapeDtypeStruct((BLOCK, BLO...]
where the time goes in v6:
time: 63.6 us; the launch traced here: 63.5 us
  Pallas kernels  63.5 us (100%)
    pallas_call x1, Pallas kernels, gather(): pl.pallas_call(gather_kernel, out_shape=(jax.ShapeDtypeStruct((BLOCK, BLO...  57.5 us
    pallas_call x1, Pallas kernels, tiles(): pl.pallas_call(tile_kernel, out_shape=jax.ShapeDtypeStruct((1, 2, BLOCK,...  6.02 us

profile of v6, /device:TPU:1, one launch (start us, length us, event | category | flops | bytes accessed | tf_op | source)
XLA Modules:
  0.0 63.5 jit_solution(4785140903254138095)
XLA Ops:
  0.0 57.5 %gather_panels.1 = (bf16[2048,2048]{1,0:T(8,128)(2,1)S(1)}, bf16[2,2048,512]{2,1,0:T(8,128)(2,1)S(1)}) custom-call(s32[256,512]{1,0:T(8,128)} %counts_hbm.1, s32[4,128]{1,0:T(4,128)} %bitcast.3, s32[18,128]{1,0:T(8,128)} %constant.2.clone.table_hbm), custom_call_target="tpu_custom_call" | custom-call | tf_op jit(solution)/shard_map/gather_panels/pallas_call | solution.py:378
  57.5 6.0 %tile_products.1 = bf16[1,2,2048,2048]{3,2,1,0:T(8,128)(2,1)} custom-call(bf16[2048,2048]{1,0:T(8,128)(2,1)S(1)} %get-tuple-element.7.tile_ref, bf16[2,2048,512]{2,1,0:T(8,128)(2,1)S(1)} %get-tuple-element.8.panels_ref), custom_call_target="tpu_custom_call" | custom-call | tf_op jit(solution)/shard_map/tile_products/pallas_call | solution.py:438

commit v7 on v5

--- a/solution.py
+++ b/solution.py
@@ -292,7 +292,7 @@
         factor = 1.0 / SNPS if panel % 2 == 0 else 1.0
 
         def message(m, carry):
-            to_core, link = m // len(LINKS), m % len(LINKS)
+            to_core, link = (core + m // len(LINKS)) % 2, m % len(LINKS)
             step = step_of(link)
             block = wanted(device_at(step, to_core), panel)
             px, py, _ = place(step)

time: 63 us -> 63 us (level)
  no operation moved by 1% of the time
where the time goes in v7:
time: 63 us; the launch traced here: 62.9 us
  Pallas kernels  62.8 us (100%)
    pallas_call x1, Pallas kernels, gather(): pl.pallas_call(gather_kernel, out_shape=(jax.ShapeDtypeStruct((BLOCK, BLO...  56.8 us
    pallas_call x1, Pallas kernels, tiles(): pl.pallas_call(tile_kernel, out_shape=jax.ShapeDtypeStruct((1, 2, BLOCK,...  6.02 us

profile of v7, /device:TPU:1, one launch (start us, length us, event | category | flops | bytes accessed | tf_op | source)
XLA Modules:
  0.0 62.9 jit_solution(15678154267248261833)
XLA Ops:
  0.0 56.8 %gather_panels.1 = (bf16[2048,2048]{1,0:T(8,128)(2,1)S(1)}, bf16[2,2048,512]{2,1,0:T(8,128)(2,1)S(1)}) custom-call(s32[256,512]{1,0:T(8,128)} %counts_hbm.1, s32[4,128]{1,0:T(4,128)} %bitcast.3, s32[18,128]{1,0:T(8,128)} %constant.2.clone.table_hbm), custom_call_target="tpu_custom_call" | custom-call | tf_op jit(solution)/shard_map/gather_panels/pallas_call | solution.py:377
  56.8 6.0 %tile_products.1 = bf16[1,2,2048,2048]{3,2,1,0:T(8,128)(2,1)} custom-call(bf16[2048,2048]{1,0:T(8,128)(2,1)S(1)} %get-tuple-element.7.tile_ref, bf16[2,2048,512]{2,1,0:T(8,128)(2,1)S(1)} %get-tuple-element.8.panels_ref), custom_call_target="tpu_custom_call" | custom-call | tf_op jit(solution)/shard_map/tile_products/pallas_call | solution.py:437

commit v8 on v7

--- a/solution.py
+++ b/solution.py
@@ -148,14 +148,14 @@
         loads[i].wait()
         quarter = counts_ref[rows].astype(jnp.float32).astype(jnp.bfloat16)
         if i < PARTS:
-            near[2, i] = quarter
+            near[4, i] = quarter
         else:
             held[i - PARTS, core] = quarter
     halves = (core, 1 - core)
 
     def swap(p, half):
         return pltpu.make_async_remote_copy(
-            src_ref=near.at[2, p],
+            src_ref=near.at[4, p],
             dst_ref=held.at[p, half],
             send_sem=twin_send.at[p],
             recv_sem=twin_recv.at[p],
@@ -262,7 +262,7 @@
 
     def to_link(link, to_core, panel, stream):
         return pltpu.make_async_remote_copy(
-            src_ref=away.at[link, to_core, panel % 2],
+            src_ref=away.at[link, to_core, panel],
             dst_ref=landed[panel].at[stream, pl.ds(link * PER_LINK, PER_LINK)],
             send_sem=link_send.at[link, to_core, panel],
             recv_sem=link_recv.at[link, stream, panel],
@@ -272,7 +272,7 @@
 
     def to_twin(panel, stream):
         return pltpu.make_async_remote_copy(
-            src_ref=near.at[panel % 2],
+            src_ref=near.at[panel],
             dst_ref=landed[panel].at[stream, pl.ds(FROM_LINKS, OWN)],
             send_sem=near_send.at[panel],
             recv_sem=near_recv.at[panel],
@@ -287,8 +287,6 @@
         to_twin(panel, core).wait_send()
 
     def send_panel(panel):
-        if panel >= 2:
-            sent(panel - 2)
         factor = 1.0 / SNPS if panel % 2 == 0 else 1.0
 
         def message(m, carry):
@@ -299,7 +297,7 @@
             kind = kind_of(block, px, py)
             for i in range(PER_LINK):
                 slot = table_ref[kind, link * PER_LINK + i]
-                away[link, to_core, panel % 2, i] = standard(slot, block & 1, factor)
+                away[link, to_core, panel, i] = standard(slot, block & 1, factor)
             to_link(link, to_core, panel, core).start()
             return carry
 
@@ -311,7 +309,7 @@
             def one(i, carry):
                 piece = standard(table_ref[kind, FROM_LINKS + i], block & 1, factor)
                 if device is twin:
-                    near[panel % 2, i] = piece
+                    near[panel, i] = piece
                 else:
                     landed[panel][core, FROM_LINKS + i] = piece
                 return carry
@@ -367,7 +365,7 @@
     lax.fori_loop(0, BLOCK // CHUNK, multiply, 0)
     in_order(2, panels_ref.at[0])
     in_order(3, panels_ref.at[1])
-    for panel in (2, 3):
+    for panel in range(PANELS):
         sent(panel)
 
 
@@ -388,8 +386,8 @@
             pltpu.SMEM(TABLE.shape, jnp.int32),
             pltpu.VMEM((len(HELD), 2, PIECE, SNPS), bf16),
             pltpu.VMEM((15, 8, SNPS), jnp.int32),
-            pltpu.VMEM((len(LINKS), 2, 2, PER_LINK, PIECE, SNPS), bf16),
-            pltpu.VMEM((3, OWN, PIECE, SNPS), bf16),
+            pltpu.VMEM((len(LINKS), 2, PANELS, PER_LINK, PIECE, SNPS), bf16),
+            pltpu.VMEM((PANELS + 1, OWN, PIECE, SNPS), bf16),
             *[pltpu.VMEM((STREAMS, PIECES, PIECE, SNPS), bf16) for _ in range(PANELS)],
             pltpu.VMEM((BLOCK, SNPS), bf16),
             pltpu.VMEM((BLOCK, SNPS), bf16),
@@ -407,7 +405,7 @@
         ],
         name="gather_panels",
         compiler_params=pltpu.CompilerParams(
-            collective_id=0, has_side_effects=True, vmem_limit_bytes=36 * 2**20
+            collective_id=0, has_side_effects=True, vmem_limit_bytes=40 * 2**20
         ),
     )(*(pltpu.with_memory_space_constraint(a, pltpu.HBM) for a in (counts, pairs, jnp.asarray(TABLE))))
 

time: 63 us -> 63 us (level)
  no operation moved by 1% of the time
where the time goes in v8:
time: 63 us; the launch traced here: 62.9 us
  Pallas kernels  62.9 us (100%)
    pallas_call x1, Pallas kernels, gather(): pl.pallas_call(gather_kernel, out_shape=(jax.ShapeDtypeStruct((BLOCK, BLO...  56.9 us
    pallas_call x1, Pallas kernels, tiles(): pl.pallas_call(tile_kernel, out_shape=jax.ShapeDtypeStruct((1, 2, BLOCK,...  6.02 us

profile of v8, /device:TPU:1, one launch (start us, length us, event | category | flops | bytes accessed | tf_op | source)
XLA Modules:
  0.0 62.9 jit_solution(4884991692628748764)
XLA Ops:
  0.0 56.9 %gather_panels.1 = (bf16[2048,2048]{1,0:T(8,128)(2,1)S(1)}, bf16[2,2048,512]{2,1,0:T(8,128)(2,1)S(1)}) custom-call(s32[256,512]{1,0:T(8,128)} %counts_hbm.1, s32[4,128]{1,0:T(4,128)} %bitcast.3, s32[18,128]{1,0:T(8,128)} %constant.2.clone.table_hbm), custom_call_target="tpu_custom_call" | custom-call | tf_op jit(solution)/shard_map/gather_panels/pallas_call | solution.py:375
  56.9 6.0 %tile_products.1 = bf16[1,2,2048,2048]{3,2,1,0:T(8,128)(2,1)} custom-call(bf16[2048,2048]{1,0:T(8,128)(2,1)S(1)} %get-tuple-element.7.tile_ref, bf16[2,2048,512]{2,1,0:T(8,128)(2,1)S(1)} %get-tuple-element.8.panels_ref), custom_call_target="tpu_custom_call" | custom-call | tf_op jit(solution)/shard_map/tile_products/pallas_call | solution.py:435
